TPU v7x, 512 devices: a whole 4x4x16 slice. The times are simulated.
512 devices in a mesh: gx: 16 (over z), gy: 4 (over x), gz: 8 (over y, core).
Axes of the slice: x: 4, y: 4, z: 16, core: 2. Of those that a mesh axis runs over, the one named last changes fastest.
Arguments:
- species_field: float32 [11, 512, 16, 1024], P(None, 'gx', 'gy', 'gz'), may hold values from -24 to 24
- start_basis: float32 [512, 112], replicated, may hold values from -0.5 to 0.5
Outputs:
- subspace: float32 [512, 112], replicated
- core_field: float32 [112, 11, 16, 1024], P('gx', None, 'gy', 'gz')
All inputs are finite; a program needn't handle non-finite values.
Results may differ from a plain program's by a relative error of at most 0.0003.
Values sent between devices are 32-bit elements; how exact they have to be, the bound alone decides.
A program may use at most 64 MiB of HBM per device.

v0:
```python
import functools

import jax
import jax.numpy as jnp
from jax import lax
from jax.experimental import pallas as pl
from jax.experimental.pallas import tpu as pltpu
from jax.sharding import PartitionSpec as P

ITERS = 8
MESH = pl.DeviceIdType.MESH
F32 = jnp.float32
BF16 = jnp.bfloat16

Z = 16
GROUPS = 44
SLOTS = 3
CHIPS = 16


def place():
    z = lax.axis_index("gx")
    x = lax.axis_index("gy")
    w = lax.axis_index("gz")
    core = lax.rem(w, 2)
    return z, x, lax.div(w, 2), core


def first_group(dest, core):
    return 3 * dest - lax.div(dest + 3 - 2 * core, 4)


def short(dest, core):
    return lax.rem(dest, 4) == 2 * core


def partner(me, step):
    half = lax.div(step + 1, 2)
    k = 8 + half * (2 * lax.rem(step, 2) - 1)
    return lax.rem(me + k, Z)


def wait_bytes(ref, sem):
    pltpu.make_async_copy(ref, ref, sem).wait()


def split(v):
    hi = v.astype(BF16)
    return hi, (v - hi.astype(F32)).astype(BF16)


def dot_t(a, b):
    return lax.dot_general(a, b, (((1,), (1,)), ((), ())), preferred_element_type=F32)


def gram_kernel(total, x_ref, xt_out, g_out, send, recv, hi_ref, lo_ref, part, sib, half, spread,
                unit_in, unit, chunk, mine, fin, ssem, rsem, lsem):
    z, x, y, core = place()
    q = x * 4 + y
    barrier = pltpu.get_barrier_semaphore()

    def greet(step, carry):
        pl.semaphore_signal(barrier, inc=1, device_id={"gx": partner(z, step)}, device_id_type=MESH)
        p = lax.rem(q + step + 1, CHIPS)
        pl.semaphore_signal(
            barrier, inc=1, device_id={"gy": lax.div(p, 4), "gz": lax.rem(p, 4) * 2 + core}, device_id_type=MESH
        )
        return carry

    lax.fori_loop(0, 15, greet, 0)
    sibling = {"gz": y * 2 + 1 - core}
    pl.semaphore_signal(barrier, inc=1, device_id=sibling, device_id_type=MESH)

    for g in range(GROUPS):
        s, yy = divmod(g, 4)
        send[g] = x_ref[s, pl.ds(yy, 32, stride=4), :]
    pl.semaphore_wait(barrier, 31)

    rows = pl.ds(pl.multiple_of(z * 32, 32), 32)

    def copy_to(slot, d):
        return pltpu.make_async_remote_copy(
            src_ref=send.at[first_group(d, core) + slot],
            dst_ref=recv.at[slot, rows],
            send_sem=ssem.at[slot],
            recv_sem=rsem.at[slot],
            device_id={"gx": d},
            device_id_type=MESH,
        )

    for slot in range(SLOTS):
        def push(step, carry, slot=slot):
            d = partner(z, step)
            if slot < 2:
                copy_to(slot, d).start()
            else:
                @pl.when(jnp.logical_not(short(d, core)))
                def _():
                    copy_to(slot, d).start()
            return carry

        lax.fori_loop(0, 15, push, 0)
    mine_first = first_group(z, core)
    recv[0, rows] = send[mine_first]
    recv[1, rows] = send[mine_first + 1]
    is_short = short(z, core)

    @pl.when(is_short)
    def _():
        recv[2] = jnp.zeros((512, 128), F32)

    @pl.when(jnp.logical_not(is_short))
    def _():
        recv[2, rows] = send[mine_first + 2]

    others = pl.ds(0, 480)

    def accumulate(lanes, first):
        for i in range(4):
            ri = slice(128 * i, 128 * i + 128)
            up = slice(0, 128 * i + 128)
            hi_i, lo_i = hi_ref[ri, lanes], lo_ref[ri, lanes]
            hi_u = hi_ref[up, lanes]
            block = dot_t(hi_i, hi_u) + dot_t(hi_i, lo_ref[up, lanes]) + dot_t(lo_i, hi_u)
            for j in range(i + 1):
                b = i * (i + 1) // 2 + j
                rb = slice(128 * b, 128 * b + 128)
                piece = block[:, 128 * j:128 * j + 128]
                part[rb] = piece if first else part[rb] + piece

    def take(slot):
        hi, lo = split(recv[slot])
        hi_ref[:, 128 * slot:128 * slot + 128] = hi
        lo_ref[:, 128 * slot:128 * slot + 128] = lo

    wait_bytes(recv.at[0, others], rsem.at[0])
    take(0)
    wait_bytes(recv.at[1, others], rsem.at[1])
    take(1)
    accumulate(slice(0, 256), True)

    @pl.when(jnp.logical_not(is_short))
    def _():
        wait_bytes(recv.at[2, others], rsem.at[2])

    take(2)
    accumulate(slice(256, 384), False)
    keep = pltpu.make_async_copy(recv, xt_out, lsem)
    keep.start()

    own_half = pl.ds(pl.multiple_of(core * 640, 8), 640)
    other_half = pl.ds(pl.multiple_of((1 - core) * 640, 8), 640)
    swap = pltpu.make_async_remote_copy(
        src_ref=part.at[other_half], dst_ref=sib, send_sem=ssem.at[3], recv_sem=rsem.at[3],
        device_id=sibling, device_id_type=MESH)
    swap.start()
    swap.wait_recv()
    half[...] = part[own_half] + sib[...]

    def spread_to(step, carry):
        p = lax.rem(q + step + 1, CHIPS)
        pltpu.make_async_remote_copy(
            src_ref=half.at[pl.ds(pl.multiple_of(40 * p, 8), 40)], dst_ref=spread.at[q],
            send_sem=ssem.at[4], recv_sem=rsem.at[4],
            device_id={"gy": lax.div(p, 4), "gz": lax.rem(p, 4) * 2 + core}, device_id_type=MESH).start()
        return carry

    lax.fori_loop(0, 15, spread_to, 0)
    spread[q] = half[pl.ds(pl.multiple_of(40 * q, 8), 40)]
    wait_bytes(spread.at[pl.ds(0, 15)], rsem.at[4])
    chunk[...] = jnp.sum(spread[...], axis=0)

    is_owner = jnp.logical_and(lax.rem(z, 3) == 0, z < 15)
    own_t = lax.div(z, 3)
    for t in range(5):
        @pl.when(z != 3 * t)
        def _(t=t):
            pltpu.make_async_remote_copy(
                src_ref=chunk.at[pl.ds(8 * t, 8)], dst_ref=unit_in.at[z],
                send_sem=ssem.at[5], recv_sem=rsem.at[5],
                device_id={"gx": 3 * t}, device_id_type=MESH).start()

    @pl.when(is_owner)
    def _():
        mine_rows = pl.ds(pl.multiple_of(8 * own_t, 8), 8)
        unit_in[z] = chunk[mine_rows]
        wait_bytes(unit_in.at[pl.ds(0, 15)], rsem.at[5])
        unit[...] = jnp.sum(unit_in[...], axis=0) * (1.0 / total)

        def give(step, carry):
            pltpu.make_async_remote_copy(
                src_ref=unit, dst_ref=mine.at[mine_rows],
                send_sem=ssem.at[6], recv_sem=rsem.at[6],
                device_id={"gx": partner(z, step)}, device_id_type=MESH).start()
            return carry

        lax.fori_loop(0, 15, give, 0)
        mine[mine_rows] = unit[...]
        wait_bytes(mine.at[pl.ds(0, 32)], rsem.at[6])
        wait_bytes(unit_in.at[pl.ds(0, 15)], ssem.at[6])
        wait_bytes(chunk.at[pl.ds(0, 32)], ssem.at[5])

    @pl.when(jnp.logical_not(is_owner))
    def _():
        wait_bytes(mine, rsem.at[6])
        wait_bytes(chunk, ssem.at[5])

    def back_to(step, carry):
        p = lax.rem(q + step + 1, CHIPS)
        pltpu.make_async_remote_copy(
            src_ref=mine, dst_ref=fin.at[pl.ds(pl.multiple_of(core * 640 + 40 * q, 8), 40)],
            send_sem=ssem.at[7], recv_sem=rsem.at[7],
            device_id={"gy": lax.div(p, 4), "gz": lax.rem(p, 4) * 2 + core}, device_id_type=MESH).start()
        return carry

    lax.fori_loop(0, 15, back_to, 0)
    fin[pl.ds(pl.multiple_of(core * 640 + 40 * q, 8), 40)] = mine[...]
    wait_bytes(fin.at[pl.ds(0, 600)], rsem.at[7])
    swap_back = pltpu.make_async_remote_copy(
        src_ref=fin.at[own_half], dst_ref=fin.at[own_half], send_sem=ssem.at[8], recv_sem=rsem.at[8],
        device_id=sibling, device_id_type=MESH)
    swap_back.start()
    swap_back.wait_recv()

    for i in range(4):
        for j in range(i + 1):
            b = i * (i + 1) // 2 + j
            block = fin[128 * b:128 * b + 128]
            g_out[128 * i:128 * i + 128, 128 * j:128 * j + 128] = block
            if j < i:
                g_out[128 * j:128 * j + 128, 128 * i:128 * i + 128] = block.T

    wait_bytes(send.at[pl.ds(0, 15)], ssem.at[0])
    wait_bytes(send.at[pl.ds(0, 15)], ssem.at[1])

    @pl.when(is_short)
    def _():
        wait_bytes(send.at[pl.ds(0, 12)], ssem.at[2])

    @pl.when(jnp.logical_not(is_short))
    def _():
        wait_bytes(send.at[pl.ds(0, 11)], ssem.at[2])

    swap.wait_send()
    wait_bytes(half.at[pl.ds(0, 600)], ssem.at[4])
    wait_bytes(half.at[pl.ds(0, 600)], ssem.at[7])
    swap_back.wait_send()
    keep.wait()


def gram(x, total):
    vm = pl.BlockSpec(memory_space=pltpu.VMEM)
    return pl.pallas_call(
        functools.partial(gram_kernel, total),
        out_shape=(jax.ShapeDtypeStruct((SLOTS, 512, 128), F32), jax.ShapeDtypeStruct((512, 512), F32)),
        in_specs=[vm],
        out_specs=(pl.BlockSpec(memory_space=pl.ANY), vm),
        scratch_shapes=[
            pltpu.VMEM((GROUPS, 32, 128), F32),
            pltpu.VMEM((SLOTS, 512, 128), F32),
            pltpu.VMEM((512, 384), BF16),
            pltpu.VMEM((512, 384), BF16),
            pltpu.VMEM((1280, 128), F32),
            pltpu.VMEM((640, 128), F32),
            pltpu.VMEM((640, 128), F32),
            pltpu.VMEM((CHIPS, 40, 128), F32),
            pltpu.VMEM((Z, 8, 128), F32),
            pltpu.VMEM((8, 128), F32),
            pltpu.VMEM((40, 128), F32),
            pltpu.VMEM((40, 128), F32),
            pltpu.VMEM((1280, 128), F32),
            pltpu.SemaphoreType.DMA((9,)),
            pltpu.SemaphoreType.DMA((9,)),
            pltpu.SemaphoreType.DMA,
        ],
        compiler_params=pltpu.CompilerParams(
            collective_id=0, has_side_effects=True, vmem_limit_bytes=32 * 1024 * 1024),
    )(x)


RANK = 112
TILES = RANK // 8
PIECES = [(p, q, half) for p, q in ((0, 0), (0, 1), (1, 0), (0, 2), (2, 0), (1, 1)) for half in range(2)]


def spread_out(v):
    return jnp.broadcast_to(v, (8, 128))


def column(tile, k):
    return spread_out(tile[:, k:k + 1])


def row_of(ref, index, i):
    return spread_out(ref[index, i:i + 1, :])


def inverse_factor(a, work, beside):
    sub = lax.broadcasted_iota(jnp.int32, (8, 128), 0)
    lane = lax.broadcasted_iota(jnp.int32, (8, 128), 1)
    left = [a[8 * t:8 * t + 8, :] for t in range(TILES)]
    right = [(lane == sub + 8 * t).astype(F32) for t in range(TILES)]
    result = []
    ahead = None
    for t0 in range(TILES):
        k0 = 8 * t0
        base = (t0 % 2) * 18
        work[base] = left[t0]
        work[base + 1] = right[t0]
        row = [row_of(work, base, i) for i in range(8)]
        row_inv = [row_of(work, base + 1, i) for i in range(8)]
        for j in range(8):
            work[base + 2 + j] = column(left[t0], k0 + j) if ahead is None else ahead[j]
        s = [[row_of(work, base + 2 + j, i) for j in range(i + 1)] for i in range(8)]
        near = range(t0 + 1, min(TILES, t0 + 3))
        far = range(min(TILES, t0 + 3), TILES)
        col = {t: [column(left[t], k0 + j) for j in range(8)] for t in near}
        ahead = [column(left[t0 + 1], k0 + 8 + j) for j in range(8)] if near else None
        beside(t0)
        factors, inverses = [], []
        for j in range(8):
            inv = 1.0 / s[j][j]
            m = [None] * 8
            for i in range(j + 1, 8):
                m[i] = s[i][j] * inv
            factors.append(m)
            inverses.append(inv)
            for i in range(j + 1, 8):
                for n in range(j + 1, i + 1):
                    s[i][n] = s[i][n] - m[i] * s[n][j]
            for i in range(j + 1, 8):
                row[i] = row[i] - m[i] * row[j]
                row_inv[i] = row_inv[i] - m[i] * row_inv[j]
            if near:
                work[base + 10 + j] = col[t0 + 1][j]
                next_row = [row_of(work, base + 10 + j, i) for i in range(8)]
            for t in near:
                x = col[t][j] * inv
                for n in range(j + 1, 8):
                    col[t][n] = col[t][n] - x * s[n][j]
                if t == t0 + 1:
                    ahead = [ahead[n] - x * next_row[n] for n in range(8)]
                left[t] = left[t] - x * row[j]
                right[t] = right[t] - x * row_inv[j]
        tile, pivots = row_inv[7], s[7][7]
        for i in range(7):
            tile = jnp.where(sub == i, row_inv[i], tile)
            pivots = jnp.where(sub == i, s[i][i], pivots)
        result.append(tile * lax.rsqrt(pivots))
        if far:
            back, back_inv = [None] * 8, [None] * 8
            for j in reversed(range(8)):
                u, v = row[j] * inverses[j], row_inv[j] * inverses[j]
                for i in range(j + 1, 8):
                    u = u - factors[j][i] * back[i]
                    v = v - factors[j][i] * back_inv[i]
                back[j], back_inv[j] = u, v
            for t in far:
                u, v = left[t], right[t]
                for j in range(8):
                    c = column(left[t], k0 + j)
                    u = u - c * back[j]
                    v = v - c * back_inv[j]
                left[t], right[t] = u, v
    return jnp.concatenate(result, axis=0)


def split3(v):
    hi = v.astype(BF16)
    rest = v - hi.astype(F32)
    mid = rest.astype(BF16)
    return hi, mid, (rest - mid.astype(F32)).astype(BF16)


def dot_p(a, b):
    return lax.dot_general(a, b, (((1,), (0,)), ((), ())), preferred_element_type=F32)


def full(a, b, mul):
    small = (mul(a[0], b[2]) + mul(a[2], b[0])) + mul(a[1], b[1])
    return mul(a[0], b[0]) + ((mul(a[0], b[1]) + mul(a[1], b[0])) + small)


def turns_kernel(g_ref, s_ref, xt_ref, st_ref, got, image, last, ahead, inverse, parts, work, core_ref, ssem, rsem):
    z, x, y, core = place()
    barrier = pltpu.get_barrier_semaphore()

    def greet(step, carry):
        pl.semaphore_signal(barrier, inc=1, device_id={"gx": partner(z, step)}, device_id_type=MESH)
        return carry

    lax.fori_loop(0, 15, greet, 0)

    for p, part in enumerate(split3(g_ref[...])):
        parts[p] = part
    image[...] = full(split3(s_ref[...]), (parts[0], parts[1], parts[2]), dot_p)
    zeros = jnp.zeros((16, 512), BF16)

    def turn(index, carry):
        now = image[...]
        last[...] = now
        now = split3(now)
        inner = full(now, tuple(jnp.concatenate([v, zeros], axis=0) for v in now), dot_t)

        def beside(t):
            if t < len(PIECES):
                p, q, half = PIECES[t]
                lanes = slice(256 * half, 256 * half + 256)
                piece = dot_p(now[p], parts[q, :, lanes])
                ahead[:, lanes] = piece if p + q == 0 else ahead[:, lanes] + piece

        w = inverse_factor(inner, work, beside)[:, :RANK]
        inverse[...] = w
        image[...] = full(split3(w), split3(ahead[...]), dot_p)
        return carry

    lax.fori_loop(0, ITERS, turn, 0)
    basis = full(split3(inverse[...]), split3(last[...]), dot_p)
    st_ref[...] = basis
    basis_hi, basis_lo = split(basis)
    for slot in range(SLOTS):
        field_hi, field_lo = split(xt_ref[slot])
        part = dot_p(basis_hi, field_hi) + (dot_p(basis_hi, field_lo) + dot_p(basis_lo, field_hi))
        for d in range(Z):
            core_ref[d, slot] = part[7 * d:7 * d + 7, :]

    first = first_group(z, core)
    is_short = short(z, core)
    pl.semaphore_wait(barrier, 15)

    def push(n):
        def one(step, carry):
            d = partner(z, step)
            pltpu.make_async_remote_copy(
                src_ref=core_ref.at[d, pl.ds(0, n)], dst_ref=got.at[pl.ds(first, n)],
                send_sem=ssem, recv_sem=rsem, device_id={"gx": d}, device_id_type=MESH).start()
            return carry

        lax.fori_loop(0, 15, one, 0)
        got[pl.ds(first, n)] = core_ref[z, pl.ds(0, n)]
        wait_bytes(got.at[pl.ds(0, GROUPS - n)], rsem)
        wait_bytes(core_ref.at[pl.ds(0, 15), pl.ds(0, n)], ssem)

    @pl.when(is_short)
    def _():
        push(2)

    @pl.when(jnp.logical_not(is_short))
    def _():
        push(3)


def turns(g, s, xt):
    vm = pl.BlockSpec(memory_space=pltpu.VMEM)
    return pl.pallas_call(
        turns_kernel,
        out_shape=(jax.ShapeDtypeStruct((RANK, 512), F32), jax.ShapeDtypeStruct((GROUPS, 7, 128), F32)),
        in_specs=[vm, vm, vm],
        out_specs=(vm, vm),
        scratch_shapes=[
            pltpu.VMEM((RANK, 512), F32),
            pltpu.VMEM((RANK, 512), F32),
            pltpu.VMEM((RANK, 512), F32),
            pltpu.VMEM((RANK, RANK), F32),
            pltpu.VMEM((3, 512, 512), BF16),
            pltpu.VMEM((36, 8, 128), F32),
            pltpu.VMEM((Z, SLOTS, 7, 128), F32),
            pltpu.SemaphoreType.DMA,
            pltpu.SemaphoreType.DMA,
        ],
        compiler_params=pltpu.CompilerParams(
            collective_id=1, has_side_effects=True, vmem_limit_bytes=32 * 1024 * 1024),
    )(g, s, xt)


def unpack_kernel(st_ref, got_ref, st_out, core_out):
    st_out[...] = st_ref[...]
    for e in range(7):
        for s in range(11):
            core_out[e, s] = got_ref[4 * s:4 * s + 4, e, :]


def unpack(st, got):
    vm = pl.BlockSpec(memory_space=pltpu.VMEM)
    return pl.pallas_call(
        unpack_kernel,
        out_shape=(jax.ShapeDtypeStruct((RANK, 512), F32), jax.ShapeDtypeStruct((7, 11, 4, 128), F32)),
        in_specs=[vm, vm],
        out_specs=(vm, vm),
    )(st, got)


def per_device(species_field, start_basis):
    total = float(11 * 16 * 1024)
    xt, gram_matrix = gram(species_field.reshape(11, 128, 128), total)
    st, core = unpack(*turns(gram_matrix, start_basis.T, xt))
    return (st.T, core)


def solution(mesh):
    placed = (P(None, "gx", "gy", "gz"), P())
    return jax.shard_map(
        per_device,
        mesh=mesh,
        in_specs=placed,
        out_specs=(P(), P("gx", None, "gy", "gz")),
        check_vma=False,
    )
```

profile of v0, /device:TPU:1, one launch (start us, length us, event | category | flops | bytes accessed | tf_op | source)
XLA Modules:
  0.0 125.4 jit_solution(2173284277132425840)
XLA Ops:
  0.6 0.0 copy-start
  0.6 1.1 copy-done
  1.7 0.0 copy-start.2
  1.7 80.7 %shard_map.41 = (f32[3,512,128]{2,1,0:T(8,128)S(1)}, f32[512,512]{1,0:T(8,128)S(1)}) custom-call(f32[11,128,128]{2,1,0:T(8,128)S(1)} %bitcast.3), custom_call_target="tpu_custom_call" | custom-call | tf_op jit(solution)/shard_map/pallas_call | solution.py:253
  82.5 0.0 copy-done.2
  82.5 39.6 %shard_map.42 = (f32[112,512]{1,0:T(8,128)S(1)}, f32[44,7,128]{2,1,0:T(8,128)S(1)}) custom-call(f32[512,512]{1,0:T(8,128)S(1)} %get-tuple-element.8.g_ref, f32[112,512]{1,0:T(8,128)S(1)} %bitcast.4, f32[3,512,128]{2,1,0:T(8,128)S(1)} %get-tuple-element.9.xt_ref), custom_call_target="tpu_custom_call" | custom-call | tf_op jit(solution)/shard_map/pallas_call | solution.py:455
  122.1 0.0 copy-start.1
  122.1 0.7 copy-done.1
  122.8 0.0 copy-start.3
  122.8 0.7 copy-done.3
  123.5 1.9 %shard_map.43 = (f32[112,512]{1,0:T(8,128)}, f32[7,11,4,128]{3,2,1,0:T(4,128)}) custom-call(f32[112,512]{1,0:T(8,128)} %copy-done.1, f32[44,7,128]{2,1,0:T(8,128)} %copy-done.3), custom_call_target="tpu_custom_call" | custom-call | tf_op jit(solution)/shard_map/pallas_call | solution.py:485
Async XLA Ops:
  0.6 1.1 copy-start
  1.7 80.8 %copy-start.2 = (f32[512,112]{0,1:T(8,128)S(1)}, f32[512,112]{0,1:T(8,128)}, u32[]{:S(2)}) copy-start(f32[512,112]{0,1:T(8,128)} %param.3) | copy-start | bytes 688132
  122.1 0.7 copy-start.1
  122.8 0.7 copy-start.3
where the time goes:
time: 126 us; the launch traced here: 125 us
  Pallas kernels  122 us (97%)
  local copies, waits for them, and re-layouts  2.45 us (2%)
    pallas_call x1, Pallas kernels, gram(): pl.pallas_call(functools.partial(gram_kernel, total), out_shape=(jax.Shap...  80.7 us
    pallas_call x1, Pallas kernels, turns(): pl.pallas_call(turns_kernel, out_shape=(jax.ShapeDtypeStruct((RANK, 512),...  39.6 us

commit v1 on v0

--- a/solution.py
+++ b/solution.py
@@ -53,28 +53,33 @@
     return lax.dot_general(a, b, (((1,), (1,)), ((), ())), preferred_element_type=F32)
 
 
+UNITS = 5
+
+
 def gram_kernel(total, x_ref, xt_out, g_out, send, recv, hi_ref, lo_ref, part, sib, half, spread,
-                unit_in, unit, chunk, mine, fin, ssem, rsem, lsem):
+                unit_in, chunk, mine, fin, ssem, rsem, usem, lsem, token2, token3):
     z, x, y, core = place()
     q = x * 4 + y
+
+    def along_z(k):
+        return {"gx": lax.rem(z + k + Z, Z)}
+
+    def chip(p):
+        return {"gy": lax.div(p, 4), "gz": lax.rem(p, 4) * 2 + core}
+
+    sibling = {"gz": y * 2 + 1 - core}
+    close = [along_z(k) for k in (1, -1, 2, -2)] + [sibling]
+    close += [{"gy": lax.rem(x + k, 4)} for k in (1, 2, 3)]
+    close += [{"gz": lax.rem(y + k, 4) * 2 + core} for k in (1, 2, 3)]
     barrier = pltpu.get_barrier_semaphore()
-
-    def greet(step, carry):
-        pl.semaphore_signal(barrier, inc=1, device_id={"gx": partner(z, step)}, device_id_type=MESH)
-        p = lax.rem(q + step + 1, CHIPS)
-        pl.semaphore_signal(
-            barrier, inc=1, device_id={"gy": lax.div(p, 4), "gz": lax.rem(p, 4) * 2 + core}, device_id_type=MESH
-        )
-        return carry
-
-    lax.fori_loop(0, 15, greet, 0)
-    sibling = {"gz": y * 2 + 1 - core}
-    pl.semaphore_signal(barrier, inc=1, device_id=sibling, device_id_type=MESH)
-
+    for device in close:
+        pl.semaphore_signal(barrier, inc=1, device_id=device, device_id_type=MESH)
     for g in range(GROUPS):
         s, yy = divmod(g, 4)
         send[g] = x_ref[s, pl.ds(yy, 32, stride=4), :]
-    pl.semaphore_wait(barrier, 31)
+    pl.semaphore_wait(barrier, len(close))
+    for device in close:
+        pl.semaphore_signal(token2, inc=1, device_id=device, device_id_type=MESH)
 
     rows = pl.ds(pl.multiple_of(z * 32, 32), 32)
 
@@ -88,18 +93,30 @@
             device_id_type=MESH,
         )
 
+    def push(slot, k):
+        d = lax.rem(z + k + Z, Z)
+        if slot < 2:
+            copy_to(slot, d).start()
+        else:
+            @pl.when(jnp.logical_not(short(d, core)))
+            def _():
+                copy_to(slot, d).start()
+
     for slot in range(SLOTS):
-        def push(step, carry, slot=slot):
-            d = partner(z, step)
-            if slot < 2:
-                copy_to(slot, d).start()
-            else:
-                @pl.when(jnp.logical_not(short(d, core)))
-                def _():
-                    copy_to(slot, d).start()
-            return carry
-
-        lax.fori_loop(0, 15, push, 0)
+        for k in (2, -2, 1, -1):
+            push(slot, k)
+    pl.semaphore_wait(token2, len(close))
+    for k in range(1, 5):
+        for sign in (1, -1):
+            pl.semaphore_signal(token3, inc=1, device_id=along_z(sign * k), device_id_type=MESH)
+    for slot in range(SLOTS):
+        for k in (4, -4, 3, -3):
+            push(slot, k)
+    pl.semaphore_wait(token3, 8)
+    for slot in range(SLOTS):
+        for k in (8, 7, -7, 6, -6, 5, -5):
+            push(slot, k)
+
     mine_first = first_group(z, core)
     recv[0, rows] = send[mine_first]
     recv[1, rows] = send[mine_first + 1]
@@ -162,70 +179,86 @@
         pltpu.make_async_remote_copy(
             src_ref=half.at[pl.ds(pl.multiple_of(40 * p, 8), 40)], dst_ref=spread.at[q],
             send_sem=ssem.at[4], recv_sem=rsem.at[4],
-            device_id={"gy": lax.div(p, 4), "gz": lax.rem(p, 4) * 2 + core}, device_id_type=MESH).start()
+            device_id=chip(p), device_id_type=MESH).start()
         return carry
 
     lax.fori_loop(0, 15, spread_to, 0)
     spread[q] = half[pl.ds(pl.multiple_of(40 * q, 8), 40)]
     wait_bytes(spread.at[pl.ds(0, 15)], rsem.at[4])
-    chunk[...] = jnp.sum(spread[...], axis=0)
+    summed = jnp.sum(spread[...], axis=0)
+    for t in range(UNITS):
+        chunk[t] = summed[8 * t:8 * t + 8]
 
     is_owner = jnp.logical_and(lax.rem(z, 3) == 0, z < 15)
     own_t = lax.div(z, 3)
-    for t in range(5):
+    for t in range(UNITS):
         @pl.when(z != 3 * t)
         def _(t=t):
             pltpu.make_async_remote_copy(
-                src_ref=chunk.at[pl.ds(8 * t, 8)], dst_ref=unit_in.at[z],
+                src_ref=chunk.at[t], dst_ref=unit_in.at[z],
                 send_sem=ssem.at[5], recv_sem=rsem.at[5],
                 device_id={"gx": 3 * t}, device_id_type=MESH).start()
 
     @pl.when(is_owner)
     def _():
-        mine_rows = pl.ds(pl.multiple_of(8 * own_t, 8), 8)
-        unit_in[z] = chunk[mine_rows]
+        unit_in[z] = chunk[own_t]
         wait_bytes(unit_in.at[pl.ds(0, 15)], rsem.at[5])
-        unit[...] = jnp.sum(unit_in[...], axis=0) * (1.0 / total)
+        mine[own_t] = jnp.sum(unit_in[...], axis=0) * (1.0 / total)
 
         def give(step, carry):
             pltpu.make_async_remote_copy(
-                src_ref=unit, dst_ref=mine.at[mine_rows],
-                send_sem=ssem.at[6], recv_sem=rsem.at[6],
+                src_ref=mine.at[own_t], dst_ref=mine.at[own_t],
+                send_sem=ssem.at[6], recv_sem=usem.at[own_t],
                 device_id={"gx": partner(z, step)}, device_id_type=MESH).start()
             return carry
 
         lax.fori_loop(0, 15, give, 0)
-        mine[mine_rows] = unit[...]
-        wait_bytes(mine.at[pl.ds(0, 32)], rsem.at[6])
-        wait_bytes(unit_in.at[pl.ds(0, 15)], ssem.at[6])
-        wait_bytes(chunk.at[pl.ds(0, 32)], ssem.at[5])
-
-    @pl.when(jnp.logical_not(is_owner))
-    def _():
-        wait_bytes(mine, rsem.at[6])
-        wait_bytes(chunk, ssem.at[5])
-
-    def back_to(step, carry):
-        p = lax.rem(q + step + 1, CHIPS)
+
+    nearest = lax.div(z + 1, 3)
+
+    def pass_on(i, carry):
+        offset = lax.div(i + 1, 2) * (2 * lax.rem(i, 2) - 1)
+        t = lax.rem(nearest + offset + UNITS, UNITS)
+
+        @pl.when(jnp.logical_not(jnp.logical_and(is_owner, own_t == t)))
+        def _():
+            wait_bytes(mine.at[t], usem.at[t])
+
+        def back_to(step, carry):
+            p = lax.rem(q + step + 1, CHIPS)
+            pltpu.make_async_remote_copy(
+                src_ref=mine.at[t], dst_ref=fin.at[core, q, t],
+                send_sem=ssem.at[7], recv_sem=rsem.at[6 + i],
+                device_id=chip(p), device_id_type=MESH).start()
+            return carry
+
+        lax.fori_loop(0, 15, back_to, 0)
+        fin[core, q, t] = mine[t]
+        return carry
+
+    lax.fori_loop(0, UNITS, pass_on, 0)
+
+    def other_core(i, carry):
+        offset = lax.div(i + 1, 2) * (2 * lax.rem(i, 2) - 1)
+        t = lax.rem(nearest + offset + UNITS, UNITS)
+        wait_bytes(fin.at[core, pl.ds(0, 15), t], rsem.at[6 + i])
         pltpu.make_async_remote_copy(
-            src_ref=mine, dst_ref=fin.at[pl.ds(pl.multiple_of(core * 640 + 40 * q, 8), 40)],
-            send_sem=ssem.at[7], recv_sem=rsem.at[7],
-            device_id={"gy": lax.div(p, 4), "gz": lax.rem(p, 4) * 2 + core}, device_id_type=MESH).start()
+            src_ref=fin.at[core, :, t], dst_ref=fin.at[core, :, t],
+            send_sem=ssem.at[8], recv_sem=rsem.at[11],
+            device_id=sibling, device_id_type=MESH).start()
         return carry
 
-    lax.fori_loop(0, 15, back_to, 0)
-    fin[pl.ds(pl.multiple_of(core * 640 + 40 * q, 8), 40)] = mine[...]
-    wait_bytes(fin.at[pl.ds(0, 600)], rsem.at[7])
-    swap_back = pltpu.make_async_remote_copy(
-        src_ref=fin.at[own_half], dst_ref=fin.at[own_half], send_sem=ssem.at[8], recv_sem=rsem.at[8],
-        device_id=sibling, device_id_type=MESH)
-    swap_back.start()
-    swap_back.wait_recv()
+    lax.fori_loop(0, UNITS, other_core, 0)
+    wait_bytes(fin.at[1 - core], rsem.at[11])
 
     for i in range(4):
         for j in range(i + 1):
             b = i * (i + 1) // 2 + j
-            block = fin[128 * b:128 * b + 128]
+            tiles = []
+            for r in range(16 * b, 16 * b + 16):
+                h, rest = divmod(r, 80)
+                tiles.append(fin[h, rest // UNITS, rest % UNITS])
+            block = jnp.concatenate(tiles, axis=0)
             g_out[128 * i:128 * i + 128, 128 * j:128 * j + 128] = block
             if j < i:
                 g_out[128 * j:128 * j + 128, 128 * i:128 * i + 128] = block.T
@@ -243,8 +276,18 @@
 
     swap.wait_send()
     wait_bytes(half.at[pl.ds(0, 600)], ssem.at[4])
-    wait_bytes(half.at[pl.ds(0, 600)], ssem.at[7])
-    swap_back.wait_send()
+
+    @pl.when(is_owner)
+    def _():
+        wait_bytes(chunk.at[pl.ds(0, 4)], ssem.at[5])
+        wait_bytes(unit_in.at[pl.ds(0, 15)], ssem.at[6])
+
+    @pl.when(jnp.logical_not(is_owner))
+    def _():
+        wait_bytes(chunk, ssem.at[5])
+
+    wait_bytes(fin.at[core, pl.ds(0, 15)], ssem.at[7])
+    wait_bytes(fin.at[core], ssem.at[8])
     keep.wait()
 
 
@@ -265,13 +308,15 @@
             pltpu.VMEM((640, 128), F32),
             pltpu.VMEM((CHIPS, 40, 128), F32),
             pltpu.VMEM((Z, 8, 128), F32),
-            pltpu.VMEM((8, 128), F32),
-            pltpu.VMEM((40, 128), F32),
-            pltpu.VMEM((40, 128), F32),
-            pltpu.VMEM((1280, 128), F32),
+            pltpu.VMEM((UNITS, 8, 128), F32),
+            pltpu.VMEM((UNITS, 8, 128), F32),
+            pltpu.VMEM((2, CHIPS, UNITS, 8, 128), F32),
             pltpu.SemaphoreType.DMA((9,)),
-            pltpu.SemaphoreType.DMA((9,)),
+            pltpu.SemaphoreType.DMA((12,)),
+            pltpu.SemaphoreType.DMA((UNITS,)),
             pltpu.SemaphoreType.DMA,
+            pltpu.SemaphoreType.REGULAR,
+            pltpu.SemaphoreType.REGULAR,
         ],
         compiler_params=pltpu.CompilerParams(
             collective_id=0, has_side_effects=True, vmem_limit_bytes=32 * 1024 * 1024),
@@ -487,6 +532,7 @@
         out_shape=(jax.ShapeDtypeStruct((RANK, 512), F32), jax.ShapeDtypeStruct((7, 11, 4, 128), F32)),
         in_specs=[vm, vm],
         out_specs=(vm, vm),
+        compiler_params=pltpu.CompilerParams(vmem_limit_bytes=4 * 1024 * 1024),
     )(st, got)
 
 

time: 126 us -> 120 us (0.952)
  Pallas kernels: 122 us -> 118 us
  local copies, waits for them, and re-layouts: 2.45 us -> 1.11 us
    pallas_call x1, Pallas kernels: 80.7 us -> 77.8 us  [gram(): pl.pallas_call(functools.partial(gram_kernel, total), out_shape=(jax.Shap...]
    unnamed x8 -> x4, local copies, waits for them, and re-layouts: 2.45 us -> 1.11 us
where the time goes in v1:
time: 120 us
  Pallas kernels  118 us (98%)
    pallas_call x1, Pallas kernels, gram(): pl.pallas_call(functools.partial(gram_kernel, total), out_shape=(jax.Shap...  77.8 us
    pallas_call x1, Pallas kernels, turns(): pl.pallas_call(turns_kernel, out_shape=(jax.ShapeDtypeStruct((RANK, 512),...  39.3 us

profile of v1, /device:TPU:1, one launch (start us, length us, event | category | flops | bytes accessed | tf_op | source)
XLA Modules:
  0.0 119.6 jit_solution(2603458643382859019)
XLA Ops:
  0.6 0.0 copy-start
  0.6 1.1 copy-done
  1.7 0.0 copy-start.1
  1.7 77.8 %shard_map.41 = (f32[3,512,128]{2,1,0:T(8,128)S(1)}, f32[512,512]{1,0:T(8,128)S(1)}) custom-call(f32[11,128,128]{2,1,0:T(8,128)S(1)} %bitcast.3), custom_call_target="tpu_custom_call" | custom-call | tf_op jit(solution)/shard_map/pallas_call | solution.py:296
  79.5 0.0 copy-done.1
  79.5 39.3 %shard_map.42 = (f32[112,512]{1,0:T(8,128)S(1)}, f32[44,7,128]{2,1,0:T(8,128)S(1)}) custom-call(f32[512,512]{1,0:T(8,128)S(1)} %get-tuple-element.8.g_ref, f32[112,512]{1,0:T(8,128)S(1)} %bitcast.4, f32[3,512,128]{2,1,0:T(8,128)S(1)} %get-tuple-element.9.xt_ref), custom_call_target="tpu_custom_call" | custom-call | tf_op jit(solution)/shard_map/pallas_call | solution.py:500
  118.8 0.8 shard_map.43
Async XLA Ops:
  0.6 1.1 copy-start
  1.7 77.8 %copy-start.1 = (f32[512,112]{0,1:T(8,128)S(1)}, f32[512,112]{0,1:T(8,128)}, u32[]{:S(2)}) copy-start(f32[512,112]{0,1:T(8,128)} %param.3) | copy-start | bytes 688132

commit v2 on v1

--- a/solution.py
+++ b/solution.py
@@ -426,7 +426,7 @@
     return mul(a[0], b[0]) + ((mul(a[0], b[1]) + mul(a[1], b[0])) + small)
 
 
-def turns_kernel(g_ref, s_ref, xt_ref, st_ref, got, image, last, ahead, inverse, parts, work, core_ref, ssem, rsem):
+def turns_kernel(g_ref, s_ref, xt_ref, st_ref, got, image, last, ahead, ahead_parts, inverse, parts, work, core_ref, ssem, rsem):
     z, x, y, core = place()
     barrier = pltpu.get_barrier_semaphore()
 
@@ -440,12 +440,18 @@
         parts[p] = part
     image[...] = full(split3(s_ref[...]), (parts[0], parts[1], parts[2]), dot_p)
     zeros = jnp.zeros((16, 512), BF16)
+    for p in range(3):
+        ahead_parts[p, RANK:] = zeros
 
     def turn(index, carry):
         now = image[...]
         last[...] = now
-        now = split3(now)
-        inner = full(now, tuple(jnp.concatenate([v, zeros], axis=0) for v in now), dot_t)
+        hi, mid, lo = now = split3(now)
+        pair = jnp.concatenate([hi, zeros, mid, zeros], axis=0)
+        both = dot_t(pair, pair)
+        small = dot_t(lo, jnp.concatenate([hi, zeros], axis=0)) + dot_t(hi, jnp.concatenate([lo, zeros], axis=0))
+        cross = both[:RANK, 128:] + both[128:128 + RANK, :128]
+        inner = both[:RANK, :128] + (cross + (small + both[128:128 + RANK, 128:]))
 
         def beside(t):
             if t < len(PIECES):
@@ -453,10 +459,18 @@
                 lanes = slice(256 * half, 256 * half + 256)
                 piece = dot_p(now[p], parts[q, :, lanes])
                 ahead[:, lanes] = piece if p + q == 0 else ahead[:, lanes] + piece
-
-        w = inverse_factor(inner, work, beside)[:, :RANK]
-        inverse[...] = w
-        image[...] = full(split3(w), split3(ahead[...]), dot_p)
+            elif t == len(PIECES):
+                for p, part in enumerate(split3(ahead[...])):
+                    ahead_parts[p, :RANK] = part
+
+        w = inverse_factor(inner, work, beside)
+        inverse[...] = w[:, :RANK]
+        hi, mid, lo = split3(w)
+        y_hi, y_mid, y_lo = ahead_parts[0], ahead_parts[1], ahead_parts[2]
+        image[...] = dot_p(
+            jnp.concatenate([hi, mid, hi, lo, hi, mid], axis=1),
+            jnp.concatenate([y_hi, y_hi, y_mid, y_hi, y_lo, y_mid], axis=0),
+        )
         return carry
 
     lax.fori_loop(0, ITERS, turn, 0)
@@ -506,6 +520,7 @@
             pltpu.VMEM((RANK, 512), F32),
             pltpu.VMEM((RANK, 512), F32),
             pltpu.VMEM((RANK, 512), F32),
+            pltpu.VMEM((3, 128, 512), BF16),
             pltpu.VMEM((RANK, RANK), F32),
             pltpu.VMEM((3, 512, 512), BF16),
             pltpu.VMEM((36, 8, 128), F32),

time: 120 us -> 116 us (0.967)
  Pallas kernels: 118 us -> 114 us
    pallas_call x1, Pallas kernels: 39.3 us -> 35.9 us  [turns(): pl.pallas_call(turns_kernel, out_shape=(jax.ShapeDtypeStruct((RANK, 512),...]
where the time goes in v2:
time: 116 us
  Pallas kernels  114 us (98%)
    pallas_call x1, Pallas kernels, gram(): pl.pallas_call(functools.partial(gram_kernel, total), out_shape=(jax.Shap...  77.8 us
    pallas_call x1, Pallas kernels, turns(): pl.pallas_call(turns_kernel, out_shape=(jax.ShapeDtypeStruct((RANK, 512),...  35.9 us

profile of v2, /device:TPU:1, one launch (start us, length us, event | category | flops | bytes accessed | tf_op | source)
XLA Modules:
  0.0 116.2 jit_solution(12723240605507853597)
XLA Ops:
  0.6 0.0 copy-start
  0.6 1.1 copy-done
  1.7 0.0 copy-start.1
  1.7 77.8 %shard_map.41 = (f32[3,512,128]{2,1,0:T(8,128)S(1)}, f32[512,512]{1,0:T(8,128)S(1)}) custom-call(f32[11,128,128]{2,1,0:T(8,128)S(1)} %bitcast.3), custom_call_target="tpu_custom_call" | custom-call | tf_op jit(solution)/shard_map/pallas_call | solution.py:296
  79.5 0.0 copy-done.1
  79.5 35.9 %shard_map.42 = (f32[112,512]{1,0:T(8,128)S(1)}, f32[44,7,128]{2,1,0:T(8,128)S(1)}) custom-call(f32[512,512]{1,0:T(8,128)S(1)} %get-tuple-element.8.g_ref, f32[112,512]{1,0:T(8,128)S(1)} %bitcast.4, f32[3,512,128]{2,1,0:T(8,128)S(1)} %get-tuple-element.9.xt_ref), custom_call_target="tpu_custom_call" | custom-call | tf_op jit(solution)/shard_map/pallas_call | solution.py:514
  115.4 0.8 shard_map.43
Async XLA Ops:
  0.6 1.1 copy-start
  1.7 77.8 %copy-start.1 = (f32[512,112]{0,1:T(8,128)S(1)}, f32[512,112]{0,1:T(8,128)}, u32[]{:S(2)}) copy-start(f32[512,112]{0,1:T(8,128)} %param.3) | copy-start | bytes 688132

commit v3 on v2

--- a/solution.py
+++ b/solution.py
@@ -57,7 +57,7 @@
 
 
 def gram_kernel(total, x_ref, xt_out, g_out, send, recv, hi_ref, lo_ref, part, sib, half, spread,
-                unit_in, chunk, mine, fin, ssem, rsem, usem, lsem, token2, token3):
+                chunk, chunks, mine, fin, ssem, rsem, lsem, token2, token3):
     z, x, y, core = place()
     q = x * 4 + y
 
@@ -132,17 +132,19 @@
 
     others = pl.ds(0, 480)
 
-    def accumulate(lanes, first):
-        for i in range(4):
+    halves = (((0, 0, 1), (1, 0, 2), (2, 0, 2)), ((2, 2, 3), (3, 0, 4)))
+
+    def accumulate(lanes, first, which):
+        for i, j0, j1 in halves[which]:
             ri = slice(128 * i, 128 * i + 128)
-            up = slice(0, 128 * i + 128)
+            rj = slice(128 * j0, 128 * j1)
             hi_i, lo_i = hi_ref[ri, lanes], lo_ref[ri, lanes]
-            hi_u = hi_ref[up, lanes]
-            block = dot_t(hi_i, hi_u) + dot_t(hi_i, lo_ref[up, lanes]) + dot_t(lo_i, hi_u)
-            for j in range(i + 1):
+            hi_j = hi_ref[rj, lanes]
+            block = dot_t(hi_i, hi_j) + dot_t(hi_i, lo_ref[rj, lanes]) + dot_t(lo_i, hi_j)
+            for j in range(j0, j1):
                 b = i * (i + 1) // 2 + j
                 rb = slice(128 * b, 128 * b + 128)
-                piece = block[:, 128 * j:128 * j + 128]
+                piece = block[:, 128 * (j - j0):128 * (j - j0) + 128]
                 part[rb] = piece if first else part[rb] + piece
 
     def take(slot):
@@ -154,102 +156,117 @@
     take(0)
     wait_bytes(recv.at[1, others], rsem.at[1])
     take(1)
-    accumulate(slice(0, 256), True)
+    accumulate(slice(0, 256), True, 0)
+    accumulate(slice(0, 256), True, 1)
 
     @pl.when(jnp.logical_not(is_short))
     def _():
         wait_bytes(recv.at[2, others], rsem.at[2])
 
     take(2)
-    accumulate(slice(256, 384), False)
-    keep = pltpu.make_async_copy(recv, xt_out, lsem)
-    keep.start()
 
     own_half = pl.ds(pl.multiple_of(core * 640, 8), 640)
     other_half = pl.ds(pl.multiple_of((1 - core) * 640, 8), 640)
     swap = pltpu.make_async_remote_copy(
         src_ref=part.at[other_half], dst_ref=sib, send_sem=ssem.at[3], recv_sem=rsem.at[3],
         device_id=sibling, device_id_type=MESH)
-    swap.start()
+    for c in range(2):
+        @pl.when(core == c)
+        def _(c=c):
+            accumulate(slice(256, 384), False, 1 - c)
+            swap.start()
+            accumulate(slice(256, 384), False, c)
+
+    keep = pltpu.make_async_copy(recv, xt_out, lsem)
+    keep.start()
     swap.wait_recv()
-    half[...] = part[own_half] + sib[...]
+    half[...] = (part[own_half] + sib[...]).reshape(CHIPS, UNITS, 8, 128)
+
+    odd = lax.rem(z, 2)
+    even_z, odd_z = {"gx": z - odd}, {"gx": z - odd + 1}
+    source = q * 2 + odd
+
+    def for_even(p):
+        return pltpu.make_async_remote_copy(
+            src_ref=half.at[p, pl.ds(0, 3)], dst_ref=spread.at[source], send_sem=ssem.at[4], recv_sem=rsem.at[4],
+            device_id=even_z | chip(p), device_id_type=MESH)
+
+    def for_odd(p):
+        return pltpu.make_async_remote_copy(
+            src_ref=half.at[p, pl.ds(3, 2)], dst_ref=spread.at[source, pl.ds(0, 2)],
+            send_sem=ssem.at[5], recv_sem=rsem.at[5],
+            device_id=odd_z | chip(p), device_id_type=MESH)
 
     def spread_to(step, carry):
         p = lax.rem(q + step + 1, CHIPS)
-        pltpu.make_async_remote_copy(
-            src_ref=half.at[pl.ds(pl.multiple_of(40 * p, 8), 40)], dst_ref=spread.at[q],
-            send_sem=ssem.at[4], recv_sem=rsem.at[4],
-            device_id=chip(p), device_id_type=MESH).start()
+        for_even(p).start()
+        for_odd(p).start()
         return carry
 
     lax.fori_loop(0, 15, spread_to, 0)
-    spread[q] = half[pl.ds(pl.multiple_of(40 * q, 8), 40)]
-    wait_bytes(spread.at[pl.ds(0, 15)], rsem.at[4])
-    summed = jnp.sum(spread[...], axis=0)
-    for t in range(UNITS):
-        chunk[t] = summed[8 * t:8 * t + 8]
-
-    is_owner = jnp.logical_and(lax.rem(z, 3) == 0, z < 15)
-    own_t = lax.div(z, 3)
-    for t in range(UNITS):
-        @pl.when(z != 3 * t)
-        def _(t=t):
+
+    def along(k):
+        return {"gx": lax.rem(z + k + Z, Z)}
+
+    def rest(n, first, cross, sum_sem):
+        own = pl.ds(0, n)
+        spread[source, 0:n] = half[q, first:first + n]
+        cross(q).start()
+        wait_bytes(spread.at[pl.ds(0, 31), own], sum_sem)
+        chunk[0:n] = jnp.sum(spread[:, 0:n], axis=0)
+
+        for k in (8, 6, -6, 4, -4, 2, -2):
             pltpu.make_async_remote_copy(
-                src_ref=chunk.at[t], dst_ref=unit_in.at[z],
-                send_sem=ssem.at[5], recv_sem=rsem.at[5],
-                device_id={"gx": 3 * t}, device_id_type=MESH).start()
-
-    @pl.when(is_owner)
-    def _():
-        unit_in[z] = chunk[own_t]
-        wait_bytes(unit_in.at[pl.ds(0, 15)], rsem.at[5])
-        mine[own_t] = jnp.sum(unit_in[...], axis=0) * (1.0 / total)
-
-        def give(step, carry):
-            pltpu.make_async_remote_copy(
-                src_ref=mine.at[own_t], dst_ref=mine.at[own_t],
-                send_sem=ssem.at[6], recv_sem=usem.at[own_t],
-                device_id={"gx": partner(z, step)}, device_id_type=MESH).start()
-            return carry
-
-        lax.fori_loop(0, 15, give, 0)
-
-    nearest = lax.div(z + 1, 3)
-
-    def pass_on(i, carry):
-        offset = lax.div(i + 1, 2) * (2 * lax.rem(i, 2) - 1)
-        t = lax.rem(nearest + offset + UNITS, UNITS)
-
-        @pl.when(jnp.logical_not(jnp.logical_and(is_owner, own_t == t)))
-        def _():
-            wait_bytes(mine.at[t], usem.at[t])
+                src_ref=chunk.at[own], dst_ref=chunks.at[lax.div(z, 2), own],
+                send_sem=ssem.at[6], recv_sem=rsem.at[6], device_id=along(k), device_id_type=MESH).start()
+        chunks[lax.div(z, 2), 0:n] = chunk[0:n]
+        wait_bytes(chunks.at[pl.ds(0, 7), own], rsem.at[6])
+        mine[0:n] = jnp.sum(chunks[:, 0:n], axis=0) * (1.0 / total)
+
+        def back(p, z_too, sem):
+            return pltpu.make_async_remote_copy(
+                src_ref=mine.at[own], dst_ref=fin.at[core, q, pl.ds(first, n)],
+                send_sem=ssem.at[sem], recv_sem=rsem.at[sem], device_id=z_too | chip(p), device_id_type=MESH)
+
+        other_z = odd_z if first == 0 else even_z
 
         def back_to(step, carry):
             p = lax.rem(q + step + 1, CHIPS)
-            pltpu.make_async_remote_copy(
-                src_ref=mine.at[t], dst_ref=fin.at[core, q, t],
-                send_sem=ssem.at[7], recv_sem=rsem.at[6 + i],
-                device_id=chip(p), device_id_type=MESH).start()
+            back(p, other_z, 8).start()
+            back(p, {}, 7).start()
             return carry
 
         lax.fori_loop(0, 15, back_to, 0)
-        fin[core, q, t] = mine[t]
-        return carry
-
-    lax.fori_loop(0, UNITS, pass_on, 0)
-
-    def other_core(i, carry):
-        offset = lax.div(i + 1, 2) * (2 * lax.rem(i, 2) - 1)
-        t = lax.rem(nearest + offset + UNITS, UNITS)
-        wait_bytes(fin.at[core, pl.ds(0, 15), t], rsem.at[6 + i])
-        pltpu.make_async_remote_copy(
-            src_ref=fin.at[core, :, t], dst_ref=fin.at[core, :, t],
-            send_sem=ssem.at[8], recv_sem=rsem.at[11],
-            device_id=sibling, device_id_type=MESH).start()
-        return carry
-
-    lax.fori_loop(0, UNITS, other_core, 0)
-    wait_bytes(fin.at[1 - core], rsem.at[11])
+        back(q, other_z, 8).start()
+        fin[core, q, first:first + n] = mine[0:n]
+
+        def to_sibling(units):
+            return pltpu.make_async_remote_copy(
+                src_ref=fin.at[core, :, units], dst_ref=fin.at[core, :, units],
+                send_sem=ssem.at[9], recv_sem=rsem.at[9], device_id=sibling, device_id_type=MESH)
+
+        same, other = pl.ds(first, n), pl.ds(3 - first, 5 - n)
+        wait_bytes(fin.at[core, pl.ds(0, 15), same], rsem.at[7])
+        to_sibling(same).start()
+        wait_bytes(fin.at[core, :, other], rsem.at[8])
+        to_sibling(other).start()
+        wait_bytes(fin.at[1 - core], rsem.at[9])
+
+        wait_bytes(chunks.at[pl.ds(0, 7), own], ssem.at[6])
+        wait_bytes(fin.at[core, pl.ds(0, 15), same], ssem.at[7])
+        wait_bytes(fin.at[core, :, same], ssem.at[8])
+
+    @pl.when(odd == 0)
+    def _():
+        rest(3, 0, for_odd, rsem.at[4])
+        wait_bytes(half.at[pl.ds(0, 15), pl.ds(0, 3)], ssem.at[4])
+        wait_bytes(half.at[:, pl.ds(0, 2)], ssem.at[5])
+
+    @pl.when(odd == 1)
+    def _():
+        rest(2, 3, for_even, rsem.at[5])
+        wait_bytes(half.at[:, pl.ds(0, 3)], ssem.at[4])
+        wait_bytes(half.at[pl.ds(0, 15), pl.ds(0, 2)], ssem.at[5])
 
     for i in range(4):
         for j in range(i + 1):
@@ -275,19 +292,7 @@
         wait_bytes(send.at[pl.ds(0, 11)], ssem.at[2])
 
     swap.wait_send()
-    wait_bytes(half.at[pl.ds(0, 600)], ssem.at[4])
-
-    @pl.when(is_owner)
-    def _():
-        wait_bytes(chunk.at[pl.ds(0, 4)], ssem.at[5])
-        wait_bytes(unit_in.at[pl.ds(0, 15)], ssem.at[6])
-
-    @pl.when(jnp.logical_not(is_owner))
-    def _():
-        wait_bytes(chunk, ssem.at[5])
-
-    wait_bytes(fin.at[core, pl.ds(0, 15)], ssem.at[7])
-    wait_bytes(fin.at[core], ssem.at[8])
+    wait_bytes(fin.at[core], ssem.at[9])
     keep.wait()
 
 
@@ -305,15 +310,14 @@
             pltpu.VMEM((512, 384), BF16),
             pltpu.VMEM((1280, 128), F32),
             pltpu.VMEM((640, 128), F32),
-            pltpu.VMEM((640, 128), F32),
-            pltpu.VMEM((CHIPS, 40, 128), F32),
-            pltpu.VMEM((Z, 8, 128), F32),
-            pltpu.VMEM((UNITS, 8, 128), F32),
-            pltpu.VMEM((UNITS, 8, 128), F32),
+            pltpu.VMEM((CHIPS, UNITS, 8, 128), F32),
+            pltpu.VMEM((2 * CHIPS, 3, 8, 128), F32),
+            pltpu.VMEM((3, 8, 128), F32),
+            pltpu.VMEM((Z // 2, 3, 8, 128), F32),
+            pltpu.VMEM((3, 8, 128), F32),
             pltpu.VMEM((2, CHIPS, UNITS, 8, 128), F32),
-            pltpu.SemaphoreType.DMA((9,)),
-            pltpu.SemaphoreType.DMA((12,)),
-            pltpu.SemaphoreType.DMA((UNITS,)),
+            pltpu.SemaphoreType.DMA((10,)),
+            pltpu.SemaphoreType.DMA((10,)),
             pltpu.SemaphoreType.DMA,
             pltpu.SemaphoreType.REGULAR,
             pltpu.SemaphoreType.REGULAR,

time: 116 us -> 113 us (0.974)
  Pallas kernels: 114 us -> 111 us
    pallas_call x1, Pallas kernels: 77.8 us -> 74.3 us  [gram(): pl.pallas_call(functools.partial(gram_kernel, total), out_shape=(jax.Shap...]
where the time goes in v3:
time: 113 us
  Pallas kernels  111 us (98%)
    pallas_call x1, Pallas kernels, gram(): pl.pallas_call(functools.partial(gram_kernel, total), out_shape=(jax.Shap...  74.3 us
    pallas_call x1, Pallas kernels, turns(): pl.pallas_call(turns_kernel, out_shape=(jax.ShapeDtypeStruct((RANK, 512),...  35.8 us

profile of v3, /device:TPU:1, one launch (start us, length us, event | category | flops | bytes accessed | tf_op | source)
XLA Modules:
  0.0 112.7 jit_solution(8592912019851082024)
XLA Ops:
  0.6 0.0 copy-start
  0.6 1.1 copy-done
  1.7 0.0 copy-start.1
  1.7 74.3 %shard_map.41 = (f32[3,512,128]{2,1,0:T(8,128)S(1)}, f32[512,512]{1,0:T(8,128)S(1)}) custom-call(f32[11,128,128]{2,1,0:T(8,128)S(1)} %bitcast.3), custom_call_target="tpu_custom_call" | custom-call | tf_op jit(solution)/shard_map/pallas_call | solution.py:301
  76.1 0.0 copy-done.1
  76.1 35.8 %shard_map.42 = (f32[112,512]{1,0:T(8,128)S(1)}, f32[44,7,128]{2,1,0:T(8,128)S(1)}) custom-call(f32[512,512]{1,0:T(8,128)S(1)} %get-tuple-element.8.g_ref, f32[112,512]{1,0:T(8,128)S(1)} %bitcast.4, f32[3,512,128]{2,1,0:T(8,128)S(1)} %get-tuple-element.9.xt_ref), custom_call_target="tpu_custom_call" | custom-call | tf_op jit(solution)/shard_map/pallas_call | solution.py:518
  111.9 0.8 shard_map.43
Async XLA Ops:
  0.6 1.1 copy-start
  1.7 74.3 %copy-start.1 = (f32[512,112]{0,1:T(8,128)S(1)}, f32[512,112]{0,1:T(8,128)}, u32[]{:S(2)}) copy-start(f32[512,112]{0,1:T(8,128)} %param.3) | copy-start | bytes 688132

commit v4 on v3

--- a/solution.py
+++ b/solution.py
@@ -56,10 +56,12 @@
 UNITS = 5
 
 
-def gram_kernel(total, x_ref, xt_out, g_out, send, recv, hi_ref, lo_ref, part, sib, half, spread,
-                chunk, chunks, mine, fin, ssem, rsem, lsem, token2, token3):
+def gram_part(total, x_hbm, x_ref, g_ref, send, recv, hi_ref, lo_ref, part, sib, half, spread,
+              chunk, chunks, mine, fin, ssem, rsem, lsem, token2, token3):
     z, x, y, core = place()
     q = x * 4 + y
+    load = pltpu.make_async_copy(x_hbm, x_ref, lsem)
+    load.start()
 
     def along_z(k):
         return {"gx": lax.rem(z + k + Z, Z)}
@@ -74,6 +76,7 @@
     barrier = pltpu.get_barrier_semaphore()
     for device in close:
         pl.semaphore_signal(barrier, inc=1, device_id=device, device_id_type=MESH)
+    load.wait()
     for g in range(GROUPS):
         s, yy = divmod(g, 4)
         send[g] = x_ref[s, pl.ds(yy, 32, stride=4), :]
@@ -177,8 +180,6 @@
             swap.start()
             accumulate(slice(256, 384), False, c)
 
-    keep = pltpu.make_async_copy(recv, xt_out, lsem)
-    keep.start()
     swap.wait_recv()
     half[...] = (part[own_half] + sib[...]).reshape(CHIPS, UNITS, 8, 128)
 
@@ -276,9 +277,9 @@
                 h, rest = divmod(r, 80)
                 tiles.append(fin[h, rest // UNITS, rest % UNITS])
             block = jnp.concatenate(tiles, axis=0)
-            g_out[128 * i:128 * i + 128, 128 * j:128 * j + 128] = block
+            g_ref[128 * i:128 * i + 128, 128 * j:128 * j + 128] = block
             if j < i:
-                g_out[128 * j:128 * j + 128, 128 * i:128 * i + 128] = block.T
+                g_ref[128 * j:128 * j + 128, 128 * i:128 * i + 128] = block.T
 
     wait_bytes(send.at[pl.ds(0, 15)], ssem.at[0])
     wait_bytes(send.at[pl.ds(0, 15)], ssem.at[1])
@@ -293,17 +294,215 @@
 
     swap.wait_send()
     wait_bytes(fin.at[core], ssem.at[9])
-    keep.wait()
-
-
-def gram(x, total):
+
+
+RANK = 112
+TILES = RANK // 8
+PIECES = [(p, q, half) for p, q in ((0, 0), (0, 1), (1, 0), (0, 2), (2, 0), (1, 1)) for half in range(2)]
+
+
+def spread_out(v):
+    return jnp.broadcast_to(v, (8, 128))
+
+
+def column(tile, k):
+    return spread_out(tile[:, k:k + 1])
+
+
+def row_of(ref, index, i):
+    return spread_out(ref[index, i:i + 1, :])
+
+
+NEAR = 3
+
+
+def inverse_factor(a, work, beside):
+    sub = lax.broadcasted_iota(jnp.int32, (8, 128), 0)
+    lane = lax.broadcasted_iota(jnp.int32, (8, 128), 1)
+    tiles = [a[8 * t:8 * t + 8, :] for t in range(TILES)]
+    result = []
+    ahead = None
+    for t0 in range(TILES):
+        k0 = 8 * t0
+        base = (t0 % 2) * 18
+        in_block = (lane >= k0) & (lane < k0 + 8)
+        work[base] = jnp.where(in_block, (lane == sub + k0).astype(F32), tiles[t0])
+        row = [row_of(work, base, i) for i in range(8)]
+        for j in range(8):
+            work[base + 2 + j] = column(tiles[t0], k0 + j) if ahead is None else ahead[j]
+        s = [[row_of(work, base + 2 + j, i) for j in range(i + 1)] for i in range(8)]
+        near = range(t0 + 1, min(TILES, t0 + 1 + NEAR))
+        far = range(min(TILES, t0 + 1 + NEAR), TILES)
+        col = {t: [column(tiles[t], k0 + j) for j in range(8)] for t in near}
+        ahead = [column(tiles[t0 + 1], k0 + 8 + j) for j in range(8)] if near else None
+        for t in near:
+            tiles[t] = jnp.where(in_block, 0.0, tiles[t])
+        beside(t0)
+        factors, inverses = [], []
+        for j in range(8):
+            inv = 1.0 / s[j][j]
+            m = [None] * 8
+            for i in range(j + 1, 8):
+                m[i] = s[i][j] * inv
+            factors.append(m)
+            inverses.append(inv)
+            for i in range(j + 1, 8):
+                for n in range(j + 1, i + 1):
+                    s[i][n] = s[i][n] - m[i] * s[n][j]
+            for i in range(j + 1, 8):
+                row[i] = row[i] - m[i] * row[j]
+            if near:
+                work[base + 10 + j] = col[t0 + 1][j]
+                next_row = [row_of(work, base + 10 + j, i) for i in range(8)]
+            for t in near:
+                x = col[t][j] * inv
+                for n in range(j + 1, 8):
+                    col[t][n] = col[t][n] - x * s[n][j]
+                if t == t0 + 1:
+                    ahead = [ahead[n] - x * next_row[n] for n in range(8)]
+                tiles[t] = tiles[t] - x * row[j]
+        tile, pivots = row[7], s[7][7]
+        for i in range(7):
+            tile = jnp.where(sub == i, row[i], tile)
+            pivots = jnp.where(sub == i, s[i][i], pivots)
+        result.append(jnp.where(lane < k0 + 8, tile * lax.rsqrt(pivots), 0.0))
+        if far:
+            back = [None] * 8
+            for j in reversed(range(8)):
+                u = row[j] * inverses[j]
+                for i in range(j + 1, 8):
+                    u = u - factors[j][i] * back[i]
+                back[j] = u
+            for t in far:
+                u = jnp.where(in_block, 0.0, tiles[t])
+                for j in range(8):
+                    u = u - column(tiles[t], k0 + j) * back[j]
+                tiles[t] = u
+    return jnp.concatenate(result, axis=0)
+
+
+def split3(v):
+    hi = v.astype(BF16)
+    rest = v - hi.astype(F32)
+    mid = rest.astype(BF16)
+    return hi, mid, (rest - mid.astype(F32)).astype(BF16)
+
+
+def dot_p(a, b):
+    return lax.dot_general(a, b, (((1,), (0,)), ((), ())), preferred_element_type=F32)
+
+
+def full(a, b, mul):
+    small = (mul(a[0], b[2]) + mul(a[2], b[0])) + mul(a[1], b[1])
+    return mul(a[0], b[0]) + ((mul(a[0], b[1]) + mul(a[1], b[0])) + small)
+
+
+def turns_part(g_ref, s_ref, xt_ref, st_ref, got, image, last, ahead, ahead_parts, inverse, parts, work, core_ref,
+               ssem, rsem):
+    z, x, y, core = place()
+
+    for p, part in enumerate(split3(g_ref[...])):
+        parts[p] = part
+    image[...] = full(split3(s_ref[...]), (parts[0], parts[1], parts[2]), dot_p)
+    zeros = jnp.zeros((16, 512), BF16)
+    for p in range(3):
+        ahead_parts[p, RANK:] = zeros
+
+    def turn(index, carry):
+        now = image[...]
+        last[...] = now
+        hi, mid, lo = now = split3(now)
+        pair = jnp.concatenate([hi, zeros, mid, zeros], axis=0)
+        both = dot_t(pair, pair)
+        small = dot_t(lo, jnp.concatenate([hi, zeros], axis=0)) + dot_t(hi, jnp.concatenate([lo, zeros], axis=0))
+        cross = both[:RANK, 128:] + both[128:128 + RANK, :128]
+        inner = both[:RANK, :128] + (cross + (small + both[128:128 + RANK, 128:]))
+
+        def beside(t):
+            if t < len(PIECES):
+                p, q, half = PIECES[t]
+                lanes = slice(256 * half, 256 * half + 256)
+                piece = dot_p(now[p], parts[q, :, lanes])
+                ahead[:, lanes] = piece if p + q == 0 else ahead[:, lanes] + piece
+            elif t == len(PIECES):
+                for p, part in enumerate(split3(ahead[...])):
+                    ahead_parts[p, :RANK] = part
+
+        w = inverse_factor(inner, work, beside)
+        inverse[...] = w[:, :RANK]
+        hi, mid, lo = split3(w)
+        y_hi, y_mid, y_lo = ahead_parts[0], ahead_parts[1], ahead_parts[2]
+        image[...] = dot_p(
+            jnp.concatenate([hi, mid, hi, lo, hi, mid], axis=1),
+            jnp.concatenate([y_hi, y_hi, y_mid, y_hi, y_lo, y_mid], axis=0),
+        )
+        return carry
+
+    lax.fori_loop(0, ITERS, turn, 0)
+    basis = full(split3(inverse[...]), split3(last[...]), dot_p)
+    basis_hi, basis_lo = split(basis)
+
+    def project(slot):
+        field_hi, field_lo = split(xt_ref[slot])
+        part = dot_p(basis_hi, field_hi) + (dot_p(basis_hi, field_lo) + dot_p(basis_lo, field_hi))
+        for d in range(Z):
+            core_ref[d, slot] = part[7 * d:7 * d + 7, :]
+
+    first = first_group(z, core)
+    is_short = short(z, core)
+
+    def push(slot, n):
+        def one(step, carry):
+            d = partner(z, step)
+            pltpu.make_async_remote_copy(
+                src_ref=core_ref.at[d, pl.ds(slot, n)], dst_ref=got.at[pl.ds(first + slot, n)],
+                send_sem=ssem, recv_sem=rsem, device_id={"gx": d}, device_id_type=MESH).start()
+            return carry
+
+        lax.fori_loop(0, 15, one, 0)
+
+    def finish(n):
+        push(1, n - 1)
+        got[pl.ds(first, n)] = core_ref[z, pl.ds(0, n)]
+        st_ref[...] = basis
+        wait_bytes(got.at[pl.ds(0, GROUPS - n)], rsem)
+        wait_bytes(core_ref.at[pl.ds(0, 15), pl.ds(0, n)], ssem)
+
+    project(0)
+    push(0, 1)
+    project(1)
+    project(2)
+
+    @pl.when(is_short)
+    def _():
+        finish(2)
+
+    @pl.when(jnp.logical_not(is_short))
+    def _():
+        finish(3)
+
+
+def step_kernel(total, x_hbm, s_hbm, st_ref, got, s_ref, s_sem, *scratch):
+    recv, g_ref = scratch[3], scratch[1]
+    load = pltpu.make_async_copy(s_hbm, s_ref, s_sem)
+    load.start()
+    gram_part(total, x_hbm, *scratch[:19])
+    load.wait()
+    turns_part(g_ref, s_ref, recv, st_ref, got, *scratch[19:])
+
+
+def step(x, s, total):
     vm = pl.BlockSpec(memory_space=pltpu.VMEM)
     return pl.pallas_call(
-        functools.partial(gram_kernel, total),
-        out_shape=(jax.ShapeDtypeStruct((SLOTS, 512, 128), F32), jax.ShapeDtypeStruct((512, 512), F32)),
-        in_specs=[vm],
-        out_specs=(pl.BlockSpec(memory_space=pl.ANY), vm),
+        functools.partial(step_kernel, total),
+        out_shape=(jax.ShapeDtypeStruct((RANK, 512), F32), jax.ShapeDtypeStruct((GROUPS, 7, 128), F32)),
+        in_specs=[pl.BlockSpec(memory_space=pl.ANY)] * 2,
+        out_specs=(vm, vm),
         scratch_shapes=[
+            pltpu.VMEM((RANK, 512), F32),
+            pltpu.SemaphoreType.DMA,
+            pltpu.VMEM((11, 128, 128), F32),
+            pltpu.VMEM((512, 512), F32),
             pltpu.VMEM((GROUPS, 32, 128), F32),
             pltpu.VMEM((SLOTS, 512, 128), F32),
             pltpu.VMEM((512, 384), BF16),
@@ -321,206 +520,6 @@
             pltpu.SemaphoreType.DMA,
             pltpu.SemaphoreType.REGULAR,
             pltpu.SemaphoreType.REGULAR,
-        ],
-        compiler_params=pltpu.CompilerParams(
-            collective_id=0, has_side_effects=True, vmem_limit_bytes=32 * 1024 * 1024),
-    )(x)
-
-
-RANK = 112
-TILES = RANK // 8
-PIECES = [(p, q, half) for p, q in ((0, 0), (0, 1), (1, 0), (0, 2), (2, 0), (1, 1)) for half in range(2)]
-
-
-def spread_out(v):
-    return jnp.broadcast_to(v, (8, 128))
-
-
-def column(tile, k):
-    return spread_out(tile[:, k:k + 1])
-
-
-def row_of(ref, index, i):
-    return spread_out(ref[index, i:i + 1, :])
-
-
-def inverse_factor(a, work, beside):
-    sub = lax.broadcasted_iota(jnp.int32, (8, 128), 0)
-    lane = lax.broadcasted_iota(jnp.int32, (8, 128), 1)
-    left = [a[8 * t:8 * t + 8, :] for t in range(TILES)]
-    right = [(lane == sub + 8 * t).astype(F32) for t in range(TILES)]
-    result = []
-    ahead = None
-    for t0 in range(TILES):
-        k0 = 8 * t0
-        base = (t0 % 2) * 18
-        work[base] = left[t0]
-        work[base + 1] = right[t0]
-        row = [row_of(work, base, i) for i in range(8)]
-        row_inv = [row_of(work, base + 1, i) for i in range(8)]
-        for j in range(8):
-            work[base + 2 + j] = column(left[t0], k0 + j) if ahead is None else ahead[j]
-        s = [[row_of(work, base + 2 + j, i) for j in range(i + 1)] for i in range(8)]
-        near = range(t0 + 1, min(TILES, t0 + 3))
-        far = range(min(TILES, t0 + 3), TILES)
-        col = {t: [column(left[t], k0 + j) for j in range(8)] for t in near}
-        ahead = [column(left[t0 + 1], k0 + 8 + j) for j in range(8)] if near else None
-        beside(t0)
-        factors, inverses = [], []
-        for j in range(8):
-            inv = 1.0 / s[j][j]
-            m = [None] * 8
-            for i in range(j + 1, 8):
-                m[i] = s[i][j] * inv
-            factors.append(m)
-            inverses.append(inv)
-            for i in range(j + 1, 8):
-                for n in range(j + 1, i + 1):
-                    s[i][n] = s[i][n] - m[i] * s[n][j]
-            for i in range(j + 1, 8):
-                row[i] = row[i] - m[i] * row[j]
-                row_inv[i] = row_inv[i] - m[i] * row_inv[j]
-            if near:
-                work[base + 10 + j] = col[t0 + 1][j]
-                next_row = [row_of(work, base + 10 + j, i) for i in range(8)]
-            for t in near:
-                x = col[t][j] * inv
-                for n in range(j + 1, 8):
-                    col[t][n] = col[t][n] - x * s[n][j]
-                if t == t0 + 1:
-                    ahead = [ahead[n] - x * next_row[n] for n in range(8)]
-                left[t] = left[t] - x * row[j]
-                right[t] = right[t] - x * row_inv[j]
-        tile, pivots = row_inv[7], s[7][7]
-        for i in range(7):
-            tile = jnp.where(sub == i, row_inv[i], tile)
-            pivots = jnp.where(sub == i, s[i][i], pivots)
-        result.append(tile * lax.rsqrt(pivots))
-        if far:
-            back, back_inv = [None] * 8, [None] * 8
-            for j in reversed(range(8)):
-                u, v = row[j] * inverses[j], row_inv[j] * inverses[j]
-                for i in range(j + 1, 8):
-                    u = u - factors[j][i] * back[i]
-                    v = v - factors[j][i] * back_inv[i]
-                back[j], back_inv[j] = u, v
-            for t in far:
-                u, v = left[t], right[t]
-                for j in range(8):
-                    c = column(left[t], k0 + j)
-                    u = u - c * back[j]
-                    v = v - c * back_inv[j]
-                left[t], right[t] = u, v
-    return jnp.concatenate(result, axis=0)
-
-
-def split3(v):
-    hi = v.astype(BF16)
-    rest = v - hi.astype(F32)
-    mid = rest.astype(BF16)
-    return hi, mid, (rest - mid.astype(F32)).astype(BF16)
-
-
-def dot_p(a, b):
-    return lax.dot_general(a, b, (((1,), (0,)), ((), ())), preferred_element_type=F32)
-
-
-def full(a, b, mul):
-    small = (mul(a[0], b[2]) + mul(a[2], b[0])) + mul(a[1], b[1])
-    return mul(a[0], b[0]) + ((mul(a[0], b[1]) + mul(a[1], b[0])) + small)
-
-
-def turns_kernel(g_ref, s_ref, xt_ref, st_ref, got, image, last, ahead, ahead_parts, inverse, parts, work, core_ref, ssem, rsem):
-    z, x, y, core = place()
-    barrier = pltpu.get_barrier_semaphore()
-
-    def greet(step, carry):
-        pl.semaphore_signal(barrier, inc=1, device_id={"gx": partner(z, step)}, device_id_type=MESH)
-        return carry
-
-    lax.fori_loop(0, 15, greet, 0)
-
-    for p, part in enumerate(split3(g_ref[...])):
-        parts[p] = part
-    image[...] = full(split3(s_ref[...]), (parts[0], parts[1], parts[2]), dot_p)
-    zeros = jnp.zeros((16, 512), BF16)
-    for p in range(3):
-        ahead_parts[p, RANK:] = zeros
-
-    def turn(index, carry):
-        now = image[...]
-        last[...] = now
-        hi, mid, lo = now = split3(now)
-        pair = jnp.concatenate([hi, zeros, mid, zeros], axis=0)
-        both = dot_t(pair, pair)
-        small = dot_t(lo, jnp.concatenate([hi, zeros], axis=0)) + dot_t(hi, jnp.concatenate([lo, zeros], axis=0))
-        cross = both[:RANK, 128:] + both[128:128 + RANK, :128]
-        inner = both[:RANK, :128] + (cross + (small + both[128:128 + RANK, 128:]))
-
-        def beside(t):
-            if t < len(PIECES):
-                p, q, half = PIECES[t]
-                lanes = slice(256 * half, 256 * half + 256)
-                piece = dot_p(now[p], parts[q, :, lanes])
-                ahead[:, lanes] = piece if p + q == 0 else ahead[:, lanes] + piece
-            elif t == len(PIECES):
-                for p, part in enumerate(split3(ahead[...])):
-                    ahead_parts[p, :RANK] = part
-
-        w = inverse_factor(inner, work, beside)
-        inverse[...] = w[:, :RANK]
-        hi, mid, lo = split3(w)
-        y_hi, y_mid, y_lo = ahead_parts[0], ahead_parts[1], ahead_parts[2]
-        image[...] = dot_p(
-            jnp.concatenate([hi, mid, hi, lo, hi, mid], axis=1),
-            jnp.concatenate([y_hi, y_hi, y_mid, y_hi, y_lo, y_mid], axis=0),
-        )
-        return carry
-
-    lax.fori_loop(0, ITERS, turn, 0)
-    basis = full(split3(inverse[...]), split3(last[...]), dot_p)
-    st_ref[...] = basis
-    basis_hi, basis_lo = split(basis)
-    for slot in range(SLOTS):
-        field_hi, field_lo = split(xt_ref[slot])
-        part = dot_p(basis_hi, field_hi) + (dot_p(basis_hi, field_lo) + dot_p(basis_lo, field_hi))
-        for d in range(Z):
-            core_ref[d, slot] = part[7 * d:7 * d + 7, :]
-
-    first = first_group(z, core)
-    is_short = short(z, core)
-    pl.semaphore_wait(barrier, 15)
-
-    def push(n):
-        def one(step, carry):
-            d = partner(z, step)
-            pltpu.make_async_remote_copy(
-                src_ref=core_ref.at[d, pl.ds(0, n)], dst_ref=got.at[pl.ds(first, n)],
-                send_sem=ssem, recv_sem=rsem, device_id={"gx": d}, device_id_type=MESH).start()
-            return carry
-
-        lax.fori_loop(0, 15, one, 0)
-        got[pl.ds(first, n)] = core_ref[z, pl.ds(0, n)]
-        wait_bytes(got.at[pl.ds(0, GROUPS - n)], rsem)
-        wait_bytes(core_ref.at[pl.ds(0, 15), pl.ds(0, n)], ssem)
-
-    @pl.when(is_short)
-    def _():
-        push(2)
-
-    @pl.when(jnp.logical_not(is_short))
-    def _():
-        push(3)
-
-
-def turns(g, s, xt):
-    vm = pl.BlockSpec(memory_space=pltpu.VMEM)
-    return pl.pallas_call(
-        turns_kernel,
-        out_shape=(jax.ShapeDtypeStruct((RANK, 512), F32), jax.ShapeDtypeStruct((GROUPS, 7, 128), F32)),
-        in_specs=[vm, vm, vm],
-        out_specs=(vm, vm),
-        scratch_shapes=[
             pltpu.VMEM((RANK, 512), F32),
             pltpu.VMEM((RANK, 512), F32),
             pltpu.VMEM((RANK, 512), F32),
@@ -533,8 +532,8 @@
             pltpu.SemaphoreType.DMA,
         ],
         compiler_params=pltpu.CompilerParams(
-            collective_id=1, has_side_effects=True, vmem_limit_bytes=32 * 1024 * 1024),
-    )(g, s, xt)
+            collective_id=0, has_side_effects=True, vmem_limit_bytes=(64 * 1024 - 10816) * 1024),
+    )(x, s)
 
 
 def unpack_kernel(st_ref, got_ref, st_out, core_out):
@@ -557,8 +556,7 @@
 
 def per_device(species_field, start_basis):
     total = float(11 * 16 * 1024)
-    xt, gram_matrix = gram(species_field.reshape(11, 128, 128), total)
-    st, core = unpack(*turns(gram_matrix, start_basis.T, xt))
+    st, core = unpack(*step(species_field.reshape(11, 128, 128), start_basis.T, total))
     return (st.T, core)
 
 

time: 113 us -> 109 us (0.965)
  Pallas kernels: 111 us -> 109 us
    pallas_call x2 -> x1, Pallas kernels: 110 us -> 108 us  [step(): pl.pallas_call(functools.partial(step_kernel, total), out_shape=(jax.Shap...]
where the time goes in v4:
time: 109 us
  Pallas kernels  109 us (100%)
    pallas_call x1, Pallas kernels, step(): pl.pallas_call(functools.partial(step_kernel, total), out_shape=(jax.Shap...  108 us

profile of v4, /device:TPU:1, one launch (start us, length us, event | category | flops | bytes accessed | tf_op | source)
XLA Modules:
  0.0 109.2 jit_solution(12561649830613903156)
XLA Ops:
  0.6 107.7 %shard_map.41 = (f32[112,512]{1,0:T(8,128)S(1)}, f32[44,7,128]{2,1,0:T(8,128)S(1)}) custom-call(f32[11,128,128]{2,1,0:T(8,128)} %bitcast.3, f32[112,512]{1,0:T(8,128)} %bitcast.4), custom_call_target="tpu_custom_call" | custom-call | tf_op jit(solution)/shard_map/pallas_call | solution.py:496
  108.3 0.8 shard_map.42

commit v5 on v4

--- a/solution.py
+++ b/solution.py
@@ -53,6 +53,7 @@
     return lax.dot_general(a, b, (((1,), (1,)), ((), ())), preferred_element_type=F32)
 
 
+OFFSETS = [(2, 2), (2, 1), (2, 3), (1, 2), (3, 2), (2, 0), (0, 2), (1, 1), (1, 3), (3, 1), (3, 3), (1, 0), (3, 0), (0, 1), (0, 3)]
 UNITS = 5
 
 
@@ -198,13 +199,12 @@
             send_sem=ssem.at[5], recv_sem=rsem.at[5],
             device_id=odd_z | chip(p), device_id_type=MESH)
 
-    def spread_to(step, carry):
-        p = lax.rem(q + step + 1, CHIPS)
+    def others_of_layer():
+        return [lax.rem(x + ox, 4) * 4 + lax.rem(y + oy, 4) for ox, oy in OFFSETS]
+
+    for p in others_of_layer():
         for_even(p).start()
         for_odd(p).start()
-        return carry
-
-    lax.fori_loop(0, 15, spread_to, 0)
 
     def along(k):
         return {"gx": lax.rem(z + k + Z, Z)}
@@ -231,13 +231,9 @@
 
         other_z = odd_z if first == 0 else even_z
 
-        def back_to(step, carry):
-            p = lax.rem(q + step + 1, CHIPS)
+        for p in others_of_layer():
             back(p, other_z, 8).start()
             back(p, {}, 7).start()
-            return carry
-
-        lax.fori_loop(0, 15, back_to, 0)
         back(q, other_z, 8).start()
         fin[core, q, first:first + n] = mine[0:n]
 
@@ -392,18 +388,22 @@
     return lax.dot_general(a, b, (((1,), (0,)), ((), ())), preferred_element_type=F32)
 
 
-def full(a, b, mul):
-    small = (mul(a[0], b[2]) + mul(a[2], b[0])) + mul(a[1], b[1])
-    return mul(a[0], b[0]) + ((mul(a[0], b[1]) + mul(a[1], b[0])) + small)
-
-
-def turns_part(g_ref, s_ref, xt_ref, st_ref, got, image, last, ahead, ahead_parts, inverse, parts, work, core_ref,
+def long_product(a, b):
+    hi, mid, lo = a
+    b_hi, b_mid, b_lo = b
+    return dot_p(
+        jnp.concatenate([hi, mid, hi, lo, hi, mid], axis=1),
+        jnp.concatenate([b_hi, b_hi, b_mid, b_hi, b_lo, b_mid], axis=0),
+    )
+
+
+def turns_part(g_ref, s_ref, hi_ref, lo_ref, st_ref, got, image, last, ahead, ahead_parts, inverse, parts, work, core_ref,
                ssem, rsem):
     z, x, y, core = place()
 
     for p, part in enumerate(split3(g_ref[...])):
         parts[p] = part
-    image[...] = full(split3(s_ref[...]), (parts[0], parts[1], parts[2]), dot_p)
+    image[...] = long_product(split3(s_ref[...]), (parts[0], parts[1], parts[2]))
     zeros = jnp.zeros((16, 512), BF16)
     for p in range(3):
         ahead_parts[p, RANK:] = zeros
@@ -429,22 +429,22 @@
                     ahead_parts[p, :RANK] = part
 
         w = inverse_factor(inner, work, beside)
-        inverse[...] = w[:, :RANK]
-        hi, mid, lo = split3(w)
-        y_hi, y_mid, y_lo = ahead_parts[0], ahead_parts[1], ahead_parts[2]
-        image[...] = dot_p(
-            jnp.concatenate([hi, mid, hi, lo, hi, mid], axis=1),
-            jnp.concatenate([y_hi, y_hi, y_mid, y_hi, y_lo, y_mid], axis=0),
+        inverse[...] = w
+        image[...] = long_product(split3(w), (ahead_parts[0], ahead_parts[1], ahead_parts[2]))
+        return carry
+
+    lax.fori_loop(0, ITERS, turn, 0)
+    padded = tuple(jnp.concatenate([v, zeros], axis=0) for v in split3(last[...]))
+    basis = long_product(split3(inverse[...]), padded)
+    basis_hi, basis_lo = split(basis)
+
+    def project(slot):
+        lanes = slice(128 * slot, 128 * slot + 128)
+        field_hi, field_lo = hi_ref[:, lanes], lo_ref[:, lanes]
+        part = dot_p(
+            jnp.concatenate([basis_hi, basis_hi, basis_lo], axis=1),
+            jnp.concatenate([field_hi, field_lo, field_hi], axis=0),
         )
-        return carry
-
-    lax.fori_loop(0, ITERS, turn, 0)
-    basis = full(split3(inverse[...]), split3(last[...]), dot_p)
-    basis_hi, basis_lo = split(basis)
-
-    def project(slot):
-        field_hi, field_lo = split(xt_ref[slot])
-        part = dot_p(basis_hi, field_hi) + (dot_p(basis_hi, field_lo) + dot_p(basis_lo, field_hi))
         for d in range(Z):
             core_ref[d, slot] = part[7 * d:7 * d + 7, :]
 
@@ -483,12 +483,12 @@
 
 
 def step_kernel(total, x_hbm, s_hbm, st_ref, got, s_ref, s_sem, *scratch):
-    recv, g_ref = scratch[3], scratch[1]
+    g_ref, hi_ref, lo_ref = scratch[1], scratch[4], scratch[5]
     load = pltpu.make_async_copy(s_hbm, s_ref, s_sem)
     load.start()
     gram_part(total, x_hbm, *scratch[:19])
     load.wait()
-    turns_part(g_ref, s_ref, recv, st_ref, got, *scratch[19:])
+    turns_part(g_ref, s_ref, hi_ref, lo_ref, st_ref, got, *scratch[19:])
 
 
 def step(x, s, total):
@@ -524,7 +524,7 @@
             pltpu.VMEM((RANK, 512), F32),
             pltpu.VMEM((RANK, 512), F32),
             pltpu.VMEM((3, 128, 512), BF16),
-            pltpu.VMEM((RANK, RANK), F32),
+            pltpu.VMEM((RANK, 128), F32),
             pltpu.VMEM((3, 512, 512), BF16),
             pltpu.VMEM((36, 8, 128), F32),
             pltpu.VMEM((Z, SLOTS, 7, 128), F32),

time: 109 us -> 108 us (level)
  no operation moved by 1% of the time
where the time goes in v5:
time: 108 us
  Pallas kernels  108 us (100%)
    pallas_call x1, Pallas kernels, step(): pl.pallas_call(functools.partial(step_kernel, total), out_shape=(jax.Shap...  107 us

profile of v5, /device:TPU:1, one launch (start us, length us, event | category | flops | bytes accessed | tf_op | source)
XLA Modules:
  0.0 108.3 jit_solution(16279169983667615226)
XLA Ops:
  0.6 106.8 %shard_map.41 = (f32[112,512]{1,0:T(8,128)S(1)}, f32[44,7,128]{2,1,0:T(8,128)S(1)}) custom-call(f32[11,128,128]{2,1,0:T(8,128)} %bitcast.3, f32[112,512]{1,0:T(8,128)} %bitcast.4), custom_call_target="tpu_custom_call" | custom-call | tf_op jit(solution)/shard_map/pallas_call | solution.py:496
  107.4 0.8 shard_map.42

commit v6 on v5

--- a/solution.py
+++ b/solution.py
@@ -144,7 +144,8 @@
             rj = slice(128 * j0, 128 * j1)
             hi_i, lo_i = hi_ref[ri, lanes], lo_ref[ri, lanes]
             hi_j = hi_ref[rj, lanes]
-            block = dot_t(hi_i, hi_j) + dot_t(hi_i, lo_ref[rj, lanes]) + dot_t(lo_i, hi_j)
+            lo_j = lo_ref[rj, lanes]
+            block = dot_t(hi_i, hi_j) + (dot_t(hi_i, lo_j) + dot_t(lo_i, hi_j) + dot_t(lo_i, lo_j))
             for j in range(j0, j1):
                 b = i * (i + 1) // 2 + j
                 rb = slice(128 * b, 128 * b + 128)

time: 108 us -> 108 us (level)
  no operation moved by 1% of the time
where the time goes in v6:
time: 108 us
  Pallas kernels  108 us (100%)
    pallas_call x1, Pallas kernels, step(): pl.pallas_call(functools.partial(step_kernel, total), out_shape=(jax.Shap...  107 us

profile of v6, /device:TPU:1, one launch (start us, length us, event | category | flops | bytes accessed | tf_op | source)
XLA Modules:
  0.0 108.3 jit_solution(5677412906759422171)
XLA Ops:
  0.6 106.8 %shard_map.41 = (f32[112,512]{1,0:T(8,128)S(1)}, f32[44,7,128]{2,1,0:T(8,128)S(1)}) custom-call(f32[11,128,128]{2,1,0:T(8,128)} %bitcast.3, f32[112,512]{1,0:T(8,128)} %bitcast.4), custom_call_target="tpu_custom_call" | custom-call | tf_op jit(solution)/shard_map/pallas_call | solution.py:497
  107.5 0.8 shard_map.42

commit v7 on v6

--- a/solution.py
+++ b/solution.py
@@ -248,7 +248,6 @@
         to_sibling(same).start()
         wait_bytes(fin.at[core, :, other], rsem.at[8])
         to_sibling(other).start()
-        wait_bytes(fin.at[1 - core], rsem.at[9])
 
         wait_bytes(chunks.at[pl.ds(0, 7), own], ssem.at[6])
         wait_bytes(fin.at[core, pl.ds(0, 15), same], ssem.at[7])
@@ -266,17 +265,22 @@
         wait_bytes(half.at[:, pl.ds(0, 3)], ssem.at[4])
         wait_bytes(half.at[pl.ds(0, 15), pl.ds(0, 2)], ssem.at[5])
 
-    for i in range(4):
-        for j in range(i + 1):
-            b = i * (i + 1) // 2 + j
-            tiles = []
-            for r in range(16 * b, 16 * b + 16):
-                h, rest = divmod(r, 80)
-                tiles.append(fin[h, rest // UNITS, rest % UNITS])
-            block = jnp.concatenate(tiles, axis=0)
-            g_ref[128 * i:128 * i + 128, 128 * j:128 * j + 128] = block
-            if j < i:
-                g_ref[128 * j:128 * j + 128, 128 * i:128 * i + 128] = block.T
+    def assemble(which):
+        for i, j0, j1 in halves[which]:
+            for j in range(j0, j1):
+                b = i * (i + 1) // 2 + j - 5 * which
+                tiles = [fin[which, r // UNITS, r % UNITS] for r in range(16 * b, 16 * b + 16)]
+                block = jnp.concatenate(tiles, axis=0)
+                g_ref[128 * i:128 * i + 128, 128 * j:128 * j + 128] = block
+                if j < i:
+                    g_ref[128 * j:128 * j + 128, 128 * i:128 * i + 128] = block.T
+
+    for c in range(2):
+        @pl.when(core == c)
+        def _(c=c):
+            assemble(c)
+            wait_bytes(fin.at[1 - c], rsem.at[9])
+            assemble(1 - c)
 
     wait_bytes(send.at[pl.ds(0, 15)], ssem.at[0])
     wait_bytes(send.at[pl.ds(0, 15)], ssem.at[1])

time: 108 us -> 109 us (level)
  no operation moved by 1% of the time
where the time goes in v7:
time: 109 us; the launch traced here: 108 us
  Pallas kernels  108 us (99%)
    pallas_call x1, Pallas kernels, step(): pl.pallas_call(functools.partial(step_kernel, total), out_shape=(jax.Shap...  107 us

profile of v7, /device:TPU:1, one launch (start us, length us, event | category | flops | bytes accessed | tf_op | source)
XLA Modules:
  0.0 108.4 jit_solution(2015441905845668329)
XLA Ops:
  0.6 107.0 %shard_map.41 = (f32[112,512]{1,0:T(8,128)S(1)}, f32[44,7,128]{2,1,0:T(8,128)S(1)}) custom-call(f32[11,128,128]{2,1,0:T(8,128)} %bitcast.3, f32[112,512]{1,0:T(8,128)} %bitcast.4), custom_call_target="tpu_custom_call" | custom-call | tf_op jit(solution)/shard_map/pallas_call | solution.py:501
  107.6 0.8 shard_map.42
